TPU v7x, 32 devices: a whole 2x2x4 slice. The times are simulated.
32 devices in a mesh: tm: 4 (over x, core), vocab: 8 (over z, y).
Axes of the slice: x: 2, y: 2, z: 4, core: 2. Of those that a mesh axis runs over, the one named last changes fastest.
Arguments:
- frames: bfloat16 [768, 1024], P(('tm', 'vocab')), may hold values from -6 to 6
- qkv_weight: bfloat16 [1024, 3072], replicated, may hold values from -0.375 to 0.375
- attn_out_weight: bfloat16 [1024, 1024], replicated, may hold values from -0.1875 to 0.1875
- head_weight: bfloat16 [1024, 16384], P('tm', 'vocab'), may hold values from -0.5 to 0.5
- back_weight: bfloat16 [16384, 1024], P('vocab', 'tm'), may hold values from -6 to 6
Outputs:
- conditioned: bfloat16 [768, 1024], P(('tm', 'vocab'))
- log_norm: float32 [768], P(('tm', 'vocab'))
All inputs are finite; a program needn't handle non-finite values.
Results may differ from a plain program's by a relative error of at most 0.017.
The roundings to bfloat16 on the way count: a program that leaves them out, or rounds other values in their place, can miss the bound.
Values may be sent and summed in bfloat16 or wider, within the bound.
A program may use at most 128 MiB of HBM per device.

v0:
```python
import math

import jax
import jax.numpy as jnp
from jax import lax
from jax.sharding import PartitionSpec as P

HEADS = 16
HEAD_DIM = 64
WIN = 128


def passed_along(block, axis, distance):
    devices = range(lax.axis_size(axis))
    route = [(i - distance, i) for i in devices if i - distance in devices]
    return lax.ppermute(block, axis, route)


def root_norm(values):
    return values * lax.rsqrt(jnp.mean(values * values, axis=-1, keepdims=True) + 1e-06)


def body(frames, qkv_weight, attn_out_weight, head_weight, back_weight):
    frame_rows = frames.shape[0]
    model_width = frames.shape[1]
    full_head = lax.all_gather(head_weight, "tm", axis=0, tiled=True)
    normed = root_norm(frames.astype(jnp.float32)).astype(jnp.bfloat16)
    project = jnp.dot(normed, qkv_weight, preferred_element_type=jnp.float32).astype(jnp.bfloat16)
    query = project[:, :model_width].reshape(frame_rows, HEADS, HEAD_DIM)
    own_pairs = project[:, model_width:]
    hop_count = (WIN + frame_rows - 1) // frame_rows
    past_blocks = []
    for hop_step in range(1, hop_count + 1):
        past_blocks.append(passed_along(own_pairs, ("tm", "vocab"), hop_step))
    key_rows = jnp.concatenate(past_blocks[::-1] + [own_pairs], axis=0)
    key_count = key_rows.shape[0]
    key_part = key_rows[:, :model_width].reshape(key_count, HEADS, HEAD_DIM)
    value_part = key_rows[:, model_width:].reshape(key_count, HEADS, HEAD_DIM)
    device_pos = lax.axis_index(("tm", "vocab"))
    query_pos = device_pos * frame_rows + jnp.arange(frame_rows, dtype=jnp.int32)
    key_pos = (device_pos - hop_count) * frame_rows + jnp.arange(key_count, dtype=jnp.int32)
    scores = jnp.einsum(
        "qhd,khd->hqk", query, key_part, preferred_element_type=jnp.float32
    ) / math.sqrt(HEAD_DIM)
    scores = 50.0 * jnp.tanh(scores / 50.0)
    allowed = (
        (key_pos[None, :] <= query_pos[:, None])
        & (key_pos[None, :] > query_pos[:, None] - WIN)
        & (key_pos[None, :] >= 0)
    )
    expo = jnp.where(allowed[None], jnp.exp(scores), 0.0)
    weights = (expo / jnp.sum(expo, axis=-1, keepdims=True)).astype(jnp.bfloat16)
    context = jnp.einsum("hqk,khd->qhd", weights, value_part, preferred_element_type=jnp.float32)
    context = context.astype(jnp.bfloat16).reshape(frame_rows, model_width)
    hidden = (
        frames.astype(jnp.float32)
        + jnp.dot(context, attn_out_weight, preferred_element_type=jnp.float32)
    ).astype(jnp.bfloat16)
    unit = root_norm(hidden.astype(jnp.float32)).astype(jnp.bfloat16)
    logits = jnp.dot(
        lax.all_gather(unit, "vocab", axis=0, tiled=True),
        full_head,
        preferred_element_type=jnp.float32,
    )
    label_probs = jnp.exp(30.0 * jnp.tanh(logits / 30.0)).astype(jnp.bfloat16)
    local_totals = jnp.sum(label_probs.astype(jnp.float32), axis=-1)
    partial_value = jnp.dot(
        label_probs,
        lax.all_gather(back_weight, "tm", axis=1, tiled=True),
        preferred_element_type=jnp.float32,
    )
    owned_back, owned_totals = (
        lax.psum_scatter(partial_value, "vocab", scatter_dimension=0, tiled=True),
        lax.psum_scatter(local_totals, "vocab", scatter_dimension=0, tiled=True),
    )
    back_proj = owned_back / owned_totals[:, None]
    center = back_proj - jnp.mean(back_proj, axis=-1, keepdims=True)
    spread = jnp.mean(center * center, axis=-1, keepdims=True)
    conditioned = (hidden.astype(jnp.float32) + center * lax.rsqrt(spread + 1e-05)).astype(
        jnp.bfloat16
    )
    return (conditioned, jnp.log(owned_totals))


def solution(mesh):
    return jax.shard_map(
        body,
        mesh=mesh,
        in_specs=(P(("tm", "vocab"), None), P(), P(), P("tm", "vocab"), P("vocab", "tm")),
        out_specs=(P(("tm", "vocab"), None), P(("tm", "vocab"))),
        check_vma=False,
    )
```

profile of v0, /device:TPU:0, one launch (start us, length us, event | category | flops | bytes accessed | tf_op | source)
XLA Modules:
  0.0 163.1 jit_solution(375444362861337055)
XLA Ops:
  7.2 0.0 copy-start
  7.2 0.0 all-gather.3.cloned.1.call-start
  7.2 0.7 all-gather.3.cloned.1.call-update
  7.9 0.0 all-gather.5.cloned.1.call-start
  8.0 0.7 all-gather.5.cloned.1.call-update
  8.7 0.0 reduce-scatter.2.cloned.1.call-start
  8.7 0.9 fusion.13
  9.6 3.8 %convolution_convert_fusion = bf16[24,3072]{1,0:T(8,128)(2,1)S(1)} fusion(bf16[1024,3072]{1,0:T(8,128)(2,1)} %param.6, bf16[24,1024]{1,0:T(8,128)(2,1)} %param.5, f32[24]{0:T(128)S(1)} %add_rsqrt_fusion.2), kind=kOutput, calls=%fused_computation | convolution fusion | flops 151142400 | bytes 6488160 | tf_op jit(solution)/shard_map/dot_general | solution.py:28
  13.4 0.0 copy-start.1
  13.5 7.0 %collective-permute-start = (bf16[24,2048]{1,0:T(8,128)(2,1)S(1)}, bf16[24,2048]{1,0:T(8,128)(2,1)S(1)}, u32[]{:S(2)}, u32[]{:S(2)}) collective-permute-start(bf16[24,2048]{1,0:T(8,128)(2,1)S(1)} %slice.16), channel_id=1, source_target_pairs={{0,6},{1,7},{2,8},{3,9},{4,10},{5,11},{6,12},{7,13},{8,14},{9,15},... | collective-permute-start | bytes 294920 | tf_op jit(solution)/shard_map/ppermute | solution.py:16
  20.4 1.7 %collective-permute-start.1 = (bf16[24,2048]{1,0:T(8,128)(2,1)S(1)}, bf16[24,2048]{1,0:T(8,128)(2,1)S(1)}, u32[]{:S(2)}, u32[]{:S(2)}) collective-permute-start(bf16[24,2048]{1,0:T(8,128)(2,1)S(1)} %slice.16), channel_id=1, source_target_pairs={{0,5},{1,6},{2,7},{3,8},{4,9},{5,10},{6,11},{7,12},{8,13},{9,14},{... | collective-permute-start | bytes 294920 | tf_op jit(solution)/shard_map/ppermute | solution.py:16
  22.2 5.1 %collective-permute-start.2 = (bf16[24,2048]{1,0:T(8,128)(2,1)S(1)}, bf16[24,2048]{1,0:T(8,128)(2,1)S(1)}, u32[]{:S(2)}, u32[]{:S(2)}) collective-permute-start(bf16[24,2048]{1,0:T(8,128)(2,1)S(1)} %slice.16), channel_id=1, source_target_pairs={{0,4},{1,5},{2,6},{3,7},{4,8},{5,9},{6,10},{7,11},{8,12},{9,13},{1... | collective-permute-start | bytes 294920 | tf_op jit(solution)/shard_map/ppermute | solution.py:16
  27.3 1.9 %collective-permute-start.3 = (bf16[24,2048]{1,0:T(8,128)(2,1)S(1)}, bf16[24,2048]{1,0:T(8,128)(2,1)S(1)}, u32[]{:S(2)}, u32[]{:S(2)}) collective-permute-start(bf16[24,2048]{1,0:T(8,128)(2,1)S(1)} %slice.16), channel_id=1, source_target_pairs={{0,3},{1,4},{2,5},{3,6},{4,7},{5,8},{6,9},{7,10},{8,11},{9,12},{10... | collective-permute-start | bytes 294920 | tf_op jit(solution)/shard_map/ppermute | solution.py:16
  29.2 4.1 %collective-permute-start.4 = (bf16[24,2048]{1,0:T(8,128)(2,1)S(1)}, bf16[24,2048]{1,0:T(8,128)(2,1)S(1)}, u32[]{:S(2)}, u32[]{:S(2)}) collective-permute-start(bf16[24,2048]{1,0:T(8,128)(2,1)S(1)} %slice.16), channel_id=1, source_target_pairs={{0,2},{1,3},{2,4},{3,5},{4,6},{5,7},{6,8},{7,9},{8,10},{9,11},{10,... | collective-permute-start | bytes 294920 | tf_op jit(solution)/shard_map/ppermute | solution.py:16
  33.4 0.1 and_and_fusion
  33.5 0.8 reshape.133
  34.2 0.0 collective-permute-done
  34.2 3.4 %collective-permute-start.5 = (bf16[24,2048]{1,0:T(8,128)(2,1)S(1)}, bf16[24,2048]{1,0:T(8,128)(2,1)S(1)}, u32[]{:S(2)}, u32[]{:S(2)}) collective-permute-start(bf16[24,2048]{1,0:T(8,128)(2,1)S(1)} %slice.16), channel_id=1, source_target_pairs={{0,1},{1,2},{2,3},{3,4},{4,5},{5,6},{6,7},{7,8},{8,9},{9,10},{10,1... | collective-permute-start | bytes 294920 | tf_op jit(solution)/shard_map/ppermute | solution.py:16
  37.7 0.0 collective-permute-done.1
  37.7 0.0 collective-permute-done.2
  37.7 0.0 collective-permute-done.3
  37.7 0.0 collective-permute-done.4
  37.8 2.1 %collective-permute-done.5 = bf16[24,2048]{1,0:T(8,128)(2,1)S(1)} collective-permute-done((bf16[24,2048]{1,0:T(8,128)(2,1)S(1)}, bf16[24,2048]{1,0:T(8,128)(2,1)S(1)}, u32[]{:S(2)}, u32[]{:S(2)}) %collective-permute-start.5) | collective-permute-done | bytes 98336 | tf_op jit(solution)/shard_map/ppermute | solution.py:16
  39.9 0.2 copy.15
  40.1 0.2 copy.14
  40.3 1.9 %fusion.7 = f32[16,24,168]{2,1,0:T(8,128)} fusion(bf16[168,16,64]{0,2,1:T(8,128)(2,1)S(1)} %bitcast.15, pred[24,168]{1,0:T(8,128)(4,1)S(1)} %and_and_fusion, bf16[24,16,64]{2,1,0:T(8,128)(2,1)} %reshape.133), kind=kOutput, calls=%fused_computation.11 | convolution fusion | flops 8451072 | bytes 655296 | tf_op jit(solution)/shard_map/qhd,khd->hqk/dot_general | solution.py:42
  42.3 1.4 fusion.8
  43.7 0.1 reshape.135
  43.9 0.0 copy-done
  43.9 0.0 copy-done.1
  43.9 0.5 multiply_reduce_fusion.1
  44.4 0.1 multiply_convert_fusion
  44.5 32.7 %all_gather.9 = bf16[192,1024]{1,0:T(8,128)(2,1)S(1)} all-gather(bf16[24,1024]{1,0:T(8,128)(2,1)S(1)} %multiply_convert_fusion), channel_id=1, replica_groups=mesh['tm'=4,'vocab'=8] {'vocab'}, dimensions={0}, use_global_device_ids=true | all-gather | bytes 442368 | tf_op jit(solution)/shard_map/all_gather | solution.py:61
  77.2 0.0 all-gather.3.cloned.1.call-done
  77.2 3.4 %convert_reduce_fusion = (f32[192]{0:T(256)S(1)}, bf16[192,2048]{1,0:T(8,128)(2,1)S(1)}) fusion(bf16[192,1024]{1,0:T(8,128)(2,1)S(1)} %all_gather.9, bf16[1024,2048]{1,0:T(8,128)(2,1)} %all-gather.3.cloned.1.call-done), kind=kOutput, calls=%fused_computation.6 | convolution fusion | flops 807272256 | bytes 5374720 | tf_op jit(solution)/shard_map/dot_general | solution.py:60
  80.5 0.0 copy-start.2
  80.5 5.5 %all-gather.5.cloned.1.call-done = bf16[2048,1024]{1,0:T(8,128)(2,1)} async-done(((bf16[2048,256]{1,0:T(8,128)(2,1)}), bf16[2048,1024]{1,0:T(8,128)(2,1)}) %all-gather.5.cloned.1.call-update) | async-done | bytes 4194320 | tf_op jit(solution)/shard_map/all_gather | solution.py:69
  86.1 4.1 %fusion.22 = f32[192,1024]{1,0:T(8,128)} fusion(bf16[192,2048]{1,0:T(8,128)(2,1)S(1)} %get-tuple-element.9, bf16[2048,1024]{1,0:T(8,128)(2,1)} %all-gather.5.cloned.1.call-done), kind=kOutput, calls=%fused_computation.50 | convolution fusion | flops 805306368 | bytes 5767168 | tf_op jit(solution)/shard_map/dot_general | solution.py:67
  90.1 0.0 reduce-scatter.2.cloned.1.call-update
  90.1 0.0 copy-done.2
  90.2 0.6 dynamic-slice
  91.4 21.6 %all-reduce = f32[192]{0:T(256)S(1)} all-reduce(f32[192]{0:T(256)S(1)} %get-tuple-element.8), channel_id=3, replica_groups=mesh['tm'=4,'vocab'=8] {'vocab'}, use_global_device_ids=true, to_apply=%region_5.6.clone | all-reduce | flops 192 | bytes 1536
  113.0 0.6 fusion.20
  113.5 39.3 %reduce-scatter.2.cloned.1.call-done = f32[24,1024]{1,0:T(8,128)} async-done(((f32[192,1024]{1,0:T(8,128)}), f32[24,1024]{1,0:T(8,128)}) %reduce-scatter.2.cloned.1.call-update) | async-done | bytes 98320 | tf_op jit(solution)/shard_map/reduce_scatter | solution.py:73
  152.8 1.1 fusion.19
  153.9 1.1 multiply_reduce_fusion
  155.0 1.6 add_convert_fusion
  (18 shorter events, 0.2 us)
Async XLA Ops:
  7.2 36.7 %copy-start = (bf16[1024,1024]{1,0:T(8,128)(2,1)S(1)}, bf16[1024,1024]{1,0:T(8,128)(2,1)}, u32[]{:S(2)}) copy-start(bf16[1024,1024]{1,0:T(8,128)(2,1)} %param.7) | copy-start | bytes 6291460
  7.2 70.0 %all-gather.3.cloned.1.call-start = ((), (), s32[]{:S(2)}) async-start(), calls=%async_computation.1 | async-start | bytes 5242880 | tf_op jit(solution)/shard_map/all_gather | solution.py:26
  7.9 78.1 %all-gather.5.cloned.1.call-start = ((), (), s32[]{:S(2)}) async-start(), calls=%async_computation.2 | async-start | bytes 5242880 | tf_op jit(solution)/shard_map/all_gather | solution.py:69
  8.7 144.1 %reduce-scatter.2.cloned.1.call-start = ((), (), s32[]{:S(2)}) async-start(), calls=%async_computation.3 | async-start | bytes 884736 | tf_op jit(solution)/shard_map/reduce_scatter | solution.py:73
  13.4 30.4 %copy-start.1 = (bf16[24,1024]{1,0:T(8,128)(2,1)S(1)}, bf16[24,1024]{1,0:T(8,128)(2,1)}, u32[]{:S(2)}) copy-start(bf16[24,1024]{1,0:T(8,128)(2,1)} %param.5) | copy-start | bytes 147460
  13.5 20.8 %collective-permute-start = (bf16[24,2048]{1,0:T(8,128)(2,1)S(1)}, bf16[24,2048]{1,0:T(8,128)(2,1)S(1)}, u32[]{:S(2)}, u32[]{:S(2)}) collective-permute-start(bf16[24,2048]{1,0:T(8,128)(2,1)S(1)} %slice.16), channel_id=1, source_target_pairs={{0,6},{1,7},{2,8},{3,9},{4,10},{5,11},{6,12},{7,13},{8,14},{9,15},... | collective-permute-start | bytes 294920 | tf_op jit(solution)/shard_map/ppermute | solution.py:16
  20.4 17.2 %collective-permute-start.1 = (bf16[24,2048]{1,0:T(8,128)(2,1)S(1)}, bf16[24,2048]{1,0:T(8,128)(2,1)S(1)}, u32[]{:S(2)}, u32[]{:S(2)}) collective-permute-start(bf16[24,2048]{1,0:T(8,128)(2,1)S(1)} %slice.16), channel_id=1, source_target_pairs={{0,5},{1,6},{2,7},{3,8},{4,9},{5,10},{6,11},{7,12},{8,13},{9,14},{... | collective-permute-start | bytes 294920 | tf_op jit(solution)/shard_map/ppermute | solution.py:16
  22.2 15.5 %collective-permute-start.2 = (bf16[24,2048]{1,0:T(8,128)(2,1)S(1)}, bf16[24,2048]{1,0:T(8,128)(2,1)S(1)}, u32[]{:S(2)}, u32[]{:S(2)}) collective-permute-start(bf16[24,2048]{1,0:T(8,128)(2,1)S(1)} %slice.16), channel_id=1, source_target_pairs={{0,4},{1,5},{2,6},{3,7},{4,8},{5,9},{6,10},{7,11},{8,12},{9,13},{1... | collective-permute-start | bytes 294920 | tf_op jit(solution)/shard_map/ppermute | solution.py:16
  27.3 10.4 %collective-permute-start.3 = (bf16[24,2048]{1,0:T(8,128)(2,1)S(1)}, bf16[24,2048]{1,0:T(8,128)(2,1)S(1)}, u32[]{:S(2)}, u32[]{:S(2)}) collective-permute-start(bf16[24,2048]{1,0:T(8,128)(2,1)S(1)} %slice.16), channel_id=1, source_target_pairs={{0,3},{1,4},{2,5},{3,6},{4,7},{5,8},{6,9},{7,10},{8,11},{9,12},{10... | collective-permute-start | bytes 294920 | tf_op jit(solution)/shard_map/ppermute | solution.py:16
  29.2 8.6 %collective-permute-start.4 = (bf16[24,2048]{1,0:T(8,128)(2,1)S(1)}, bf16[24,2048]{1,0:T(8,128)(2,1)S(1)}, u32[]{:S(2)}, u32[]{:S(2)}) collective-permute-start(bf16[24,2048]{1,0:T(8,128)(2,1)S(1)} %slice.16), channel_id=1, source_target_pairs={{0,2},{1,3},{2,4},{3,5},{4,6},{5,7},{6,8},{7,9},{8,10},{9,11},{10,... | collective-permute-start | bytes 294920 | tf_op jit(solution)/shard_map/ppermute | solution.py:16
  34.2 5.6 %collective-permute-start.5 = (bf16[24,2048]{1,0:T(8,128)(2,1)S(1)}, bf16[24,2048]{1,0:T(8,128)(2,1)S(1)}, u32[]{:S(2)}, u32[]{:S(2)}) collective-permute-start(bf16[24,2048]{1,0:T(8,128)(2,1)S(1)} %slice.16), channel_id=1, source_target_pairs={{0,1},{1,2},{2,3},{3,4},{4,5},{5,6},{6,7},{7,8},{8,9},{9,10},{10,1... | collective-permute-start | bytes 294920 | tf_op jit(solution)/shard_map/ppermute | solution.py:16
  80.5 9.6 %copy-start.2 = (u32[32]{0:T(128)S(1)}, u32[32]{0:T(128)}, u32[]{:S(2)}) copy-start(u32[32]{0:T(128)} %constant.46) | copy-start | bytes 388
Sparse Core Ops, SparseCore 0:
  9.6 37.9 all-gather.2
  49.1 36.8 all-gather.4
  90.3 62.5 reduce-scatter.1
where the time goes:
time: 164 us; the launch traced here: 163 us
  blocking collectives  54.2 us (33%)
  waiting for transfers between devices  48.2 us (29%)
  starting transfers between devices  23.3 us (14%)
  matrix products  15.1 us (9%)
  between operations  14.7 us (9%)
  other arithmetic  4.91 us (3%)
  local copies, waits for them, and re-layouts  2.65 us (2%)
    reduce_scatter x1, waiting for transfers between devices, body(): lax.psum_scatter(partial_value, 'vocab', scatter_dimension=0, tiled=True)  39.3 us
    all_gather x1, blocking collectives, body(): lax.all_gather(unit, 'vocab', axis=0, tiled=True)  32.7 us
    ppermute x6, starting transfers between devices, passed_along(): return lax.ppermute(block, axis, route)  23.2 us
    unnamed x1, blocking collectives  21.6 us
    all_gather x1, waiting for transfers between devices, body(): lax.all_gather(back_weight, 'tm', axis=1, tiled=True)  5.51 us
    dot_general x1, matrix products, body(): jnp.dot(label_probs, lax.all_gather(back_weight, 'tm', axis=1, tiled=True...  4.05 us
    dot_general x1, matrix products, body(): jnp.dot(normed, qkv_weight, preferred_element_type=jnp.float32)  3.81 us
    dot_general x1, matrix products, body(): jnp.dot(lax.all_gather(unit, 'vocab', axis=0, tiled=True), full_head, pre...  3.37 us
  transfers between devices with their start and end apart: 9, of which 3 were waited for; matrix products, arithmetic and copies ran while one was open for 9% of the time, Pallas kernels for 0%

commit v1 on v0

v1 whole, which is shorter than its diff:
```python
import functools
import math

import jax
import jax.numpy as jnp
from jax import lax
from jax.experimental import pallas as pl
from jax.experimental.pallas import tpu as pltpu
from jax.sharding import PartitionSpec as P

HEADS = 16
HEAD_DIM = 64
WIN = 128
LANES = 128
BF16 = jnp.bfloat16
F32 = jnp.float32
MESH = pl.DeviceIdType.MESH


def root_norm(values):
    return values * lax.rsqrt(jnp.mean(values * values, axis=-1, keepdims=True) + 1e-06)


def pack(main, tot):
    lane = lax.broadcasted_iota(jnp.int32, (main.shape[0], LANES), 1)
    high = tot.astype(BF16).astype(F32)
    tail = jnp.where(lane == 0, high, jnp.where(lane == 1, tot - high, 0.0))
    return jnp.concatenate([main, tail], axis=1).astype(BF16)


def unpack(packed, width):
    wide = packed.astype(F32)
    return wide[:, :width], jnp.sum(wide[:, width:], axis=-1, keepdims=True)


def kernel(
    n_tm, n_voc, rows, width, hops, group,
    frames_ref, qkv_ref, out_ref, head_ref, back_ref,
    cond_ref, log_ref,
    fr, wq, wo, head, back, units, parts, near, sums, far, owned,
    loc_sem, halo_s, halo_r, head_s, head_r, back_s, back_r,
    voc_s, voc_r, sib_s, sib_r, far_s, far_r, near_s, near_r, sum_s, sum_r, own_s, own_r,
):
    t = lax.axis_index("tm")
    v = lax.axis_index("vocab")
    n_dev = n_tm * n_voc
    pairs = n_tm // 2
    me = t * n_voc + v
    sib = t + 1 - 2 * lax.rem(t, 2)
    depth = head_ref.shape[0]
    labels = head.shape[1]
    chunks = n_voc // group

    def remote(src, dst, ss, rs, dev):
        return pltpu.make_async_remote_copy(
            src_ref=src, dst_ref=dst, send_sem=ss, recv_sem=rs, device_id=dev, device_id_type=MESH
        )

    def other(k):
        return lax.rem(t + k, n_tm)

    def linear(i):
        return (i // n_voc, lax.rem(i, n_voc))

    def head_rows(i):
        return head.at[pl.ds(pl.multiple_of(i * depth, depth), depth)]

    def back_cols(i):
        return back.at[:, pl.ds(pl.multiple_of(i * depth, depth), depth)]

    def head_part(i):
        return head_ref.at[:, pl.ds(pl.multiple_of(i * labels, labels), labels)]

    def back_part(i):
        return back_ref.at[pl.ds(pl.multiple_of(i * labels, labels), labels)]

    local = [
        pltpu.make_async_copy(frames_ref, fr.at[hops], loc_sem.at[0]),
        pltpu.make_async_copy(qkv_ref, wq, loc_sem.at[1]),
        pltpu.make_async_copy(out_ref, wo, loc_sem.at[2]),
        pltpu.make_async_copy(head_part(t), head_rows(t), loc_sem.at[3]),
        pltpu.make_async_copy(back_part(t), back_cols(t), loc_sem.at[4]),
    ]
    for copy in local:
        copy.start()

    barrier = pltpu.get_barrier_semaphore()
    greet = lambda dev: pl.semaphore_signal(barrier, inc=1, device_id=dev, device_id_type=MESH)
    for k in range(1, n_tm):
        greet((other(k), v))
    lax.fori_loop(1, n_voc, lambda k, c: (greet((t, lax.rem(v + k, n_voc))), c)[1], 0)
    for s in range(1, hops + 1):
        @pl.when(me + s < n_dev)
        def _():
            greet(linear(me + s))

        @pl.when(me >= s)
        def _():
            greet(linear(me - s))

    pl.semaphore_wait(
        barrier,
        n_tm - 1 + n_voc - 1 + jnp.minimum(hops, me) + jnp.minimum(hops, n_dev - 1 - me),
    )

    def halo(s):
        return remote(frames_ref, fr.at[hops - s], halo_s.at[s - 1], halo_r.at[s - 1], linear(me + s))

    for s in range(1, hops + 1):
        @pl.when(me + s < n_dev)
        def _():
            halo(s).start()

        @pl.when(me < s)
        def _():
            fr[hops - s] = jnp.zeros((rows, width), BF16)

    order = [k for k in range(2, n_tm)] + [1]
    head_copies, back_copies = [], []
    for k in order:
        p = other(k)
        head_copies.append(remote(head_part(p), head_rows(t), head_s.at[k - 1], head_r.at[k - 1], (p, v)))
        back_copies.append(remote(back_part(p), back_cols(t), back_s.at[k - 1], back_r.at[k - 1], (p, v)))
    for copy in head_copies + back_copies:
        copy.start()

    local[0].wait()
    for s in range(1, hops + 1):
        @pl.when(me >= s)
        def _():
            remote(frames_ref, fr.at[hops - s], halo_s.at[s - 1], halo_r.at[s - 1], (t, v)).wait_recv()

    own = fr[hops].astype(F32)
    blocks = [fr[i].astype(F32) for i in range(hops)] + [own]
    used = (hops + 1) * rows
    keys = (used + LANES - 1) // LANES * LANES
    if keys > used:
        blocks.append(jnp.zeros((keys - used, width), F32))
    normed = root_norm(jnp.concatenate(blocks, axis=0)).astype(BF16)
    query_in = root_norm(own).astype(BF16)
    local[1].wait()
    local[2].wait()
    query = jnp.dot(query_in, wq[:, :width], preferred_element_type=F32)
    key_part = jnp.dot(normed, wq[:, width : 2 * width], preferred_element_type=F32).astype(BF16)
    value_part = jnp.dot(normed, wq[:, 2 * width :], preferred_element_type=F32).astype(BF16)
    per = LANES // HEAD_DIM
    row = lax.broadcasted_iota(jnp.int32, (rows, keys), 0)
    col = lax.broadcasted_iota(jnp.int32, (rows, keys), 1)
    gap = row + hops * rows - col
    allowed = (gap >= 0) & (gap < WIN) & (col + (me - hops) * rows >= 0)
    allowed = jnp.concatenate([allowed.astype(F32)] * per, axis=0) > 0.5
    lane = lax.broadcasted_iota(jnp.int32, (rows, LANES), 1)
    context = []
    for g in range(width // LANES):
        cols = slice(g * LANES, (g + 1) * LANES)
        q = query[:, cols]
        stacked = jnp.concatenate(
            [jnp.where(lane // HEAD_DIM == h, q, 0.0) for h in range(per)], axis=0
        ).astype(BF16)
        scores = lax.dot_general(
            stacked, key_part[:, cols], (((1,), (1,)), ((), ())), preferred_element_type=F32
        ) / math.sqrt(HEAD_DIM)
        scores = 50.0 * jnp.tanh(scores / 50.0)
        expo = jnp.where(allowed, jnp.exp(scores), 0.0)
        weights = (expo / jnp.sum(expo, axis=-1, keepdims=True)).astype(BF16)
        ctx = jnp.dot(weights, value_part[:, cols], preferred_element_type=F32)
        mixed = ctx[:rows]
        for h in range(1, per):
            mixed = jnp.where(lane // HEAD_DIM == h, ctx[h * rows : (h + 1) * rows], mixed)
        context.append(mixed)
    context = jnp.concatenate(context, axis=1).astype(BF16)
    hidden = (own + jnp.dot(context, wo[...], preferred_element_type=F32)).astype(BF16).astype(F32)
    units[t, v] = root_norm(hidden).astype(BF16)

    def voc_copy(k):
        w = lax.rem(v + k, n_voc)
        return remote(units.at[t, v], units.at[t, v], voc_s.at[k - 1], voc_r.at[k - 1], (t, w))

    def far_copy(a, w):
        return remote(
            units.at[t, w], units.at[t, w], far_s.at[a - 1, w], far_r.at[a - 1, w], (other(2 * a), v)
        )

    def sib_copy(a, w):
        o = other(2 * a)
        return remote(units.at[o, w], units.at[o, w], sib_s.at[a, w], sib_r.at[a, w], (sib, v))

    def pass_on(w):
        for a in range(1, pairs):
            far_copy(a, w).start()
        sib_copy(0, w).start()

    def loop(lo, hi, fn):
        def step(i, c):
            fn(i)
            return c

        lax.fori_loop(lo, hi, step, 0)

    loop(1, n_voc, lambda k: voc_copy(k).start())
    pass_on(v)

    def voc_arrived(k):
        voc_copy(k).wait_recv()
        pass_on(lax.rem(v + n_voc - k, n_voc))

    loop(1, n_voc, voc_arrived)

    def process(block):
        def chunk(c):
            u = jnp.concatenate(
                [units[block, c * group + j].astype(F32) for j in range(group)], axis=0
            ).astype(BF16)
            logits = jnp.dot(u, head[...], preferred_element_type=F32)
            probs = jnp.exp(30.0 * jnp.tanh(logits / 30.0)).astype(BF16)
            tot = jnp.sum(probs.astype(F32), axis=-1, keepdims=True)
            packed = pack(jnp.dot(probs, back[...], preferred_element_type=F32), tot).astype(F32)
            for j in range(group):
                parts[block, c * group + j] = packed[j * rows : (j + 1) * rows].astype(BF16)

        loop(0, chunks, chunk)

    def near_copy(a):
        return remote(parts.at[lax.rem(sib + 2 * a, n_tm)], near.at[a], near_s.at[a], near_r.at[a], (sib, v))

    local[3].wait()
    for copy in head_copies:
        copy.wait_recv()
    local[4].wait()
    for copy in back_copies:
        copy.wait_recv()
    process(t)
    for a in range(1, pairs):
        def far_arrived(k):
            w = lax.rem(v + n_voc - k, n_voc)
            far_copy(pairs - a, w).wait_recv()
            sib_copy(a, w).start()

        loop(0, n_voc, far_arrived)
    for a in range(pairs):
        if a:
            process(other(2 * a))
        loop(0, n_voc, lambda k: sib_copy(a, lax.rem(v + n_voc - k, n_voc)).wait_recv())
        process(lax.rem(sib + 2 * a, n_tm))
        near_copy(a).start()

    def sum_copy(a, w):
        return remote(
            sums.at[a - 1, w], far.at[a - 1, w], sum_s.at[a - 1, w], sum_r.at[a - 1, w], (other(2 * a), v)
        )

    for a in range(1, pairs):
        near_copy(a).wait_recv()

        def pair_sum(k):
            w = lax.rem(v + k, n_voc)
            m0, t0 = unpack(parts[other(2 * a), w], width)
            m1, t1 = unpack(near[a, w], width)
            sums[a - 1, w] = pack(m0 + m1, t0 + t1)
            sum_copy(a, w).start()

        loop(1, n_voc + 1, pair_sum)
    near_copy(0).wait_recv()

    def own_copy(k):
        w = lax.rem(v + k, n_voc)
        return remote(parts.at[t, w], owned.at[k - 1], own_s.at[k - 1], own_r.at[k - 1], (t, w))

    def tm_sum(w):
        m, s = unpack(parts[t, w], width)
        m1, s1 = unpack(near[0, w], width)
        m, s = m + m1, s + s1
        for a in range(1, pairs):
            sum_copy(a, w).wait_recv()
            m1, s1 = unpack(far[a - 1, w], width)
            m, s = m + m1, s + s1
        return m, s

    def send_sum(k):
        w = lax.rem(v + k, n_voc)
        m, s = tm_sum(w)
        parts[t, w] = pack(m, s)
        own_copy(k).start()

    loop(1, n_voc, send_sum)
    total, tot = tm_sum(v)
    for k in range(1, n_voc):
        own_copy(k).wait_recv()
        m1, s1 = unpack(owned[k - 1], width)
        total, tot = total + m1, tot + s1
    value = total / tot
    center = value - jnp.mean(value, axis=-1, keepdims=True)
    spread = jnp.mean(center * center, axis=-1, keepdims=True)
    cond_ref[...] = (hidden + center * lax.rsqrt(spread + 1e-05)).astype(BF16)
    r = lax.broadcasted_iota(jnp.int32, (rows, LANES), 0)
    c = lax.broadcasted_iota(jnp.int32, (rows, LANES), 1)
    log_ref[...] = jnp.sum(jnp.where(r == c, jnp.log(tot), 0.0), axis=0, keepdims=True)

    for s in range(1, hops + 1):
        @pl.when(me + s < n_dev)
        def _():
            halo(s).wait_send()
    for copy in head_copies + back_copies:
        copy.wait_send()
    loop(1, n_voc, lambda k: voc_copy(k).wait_send())
    loop(1, n_voc, lambda k: own_copy(k).wait_send())

    def rest(w):
        for a in range(pairs):
            sib_copy(a, w).wait_send()
            if a:
                far_copy(a, w).wait_send()
                sum_copy(a, w).wait_send()

    loop(0, n_voc, rest)
    for a in range(pairs):
        near_copy(a).wait_send()


def body(n_tm, n_voc, frames, qkv_weight, attn_out_weight, head_weight, back_weight):
    rows, width = frames.shape
    hops = (WIN + rows - 1) // rows
    labels = head_weight.shape[1] // n_tm
    pairs = n_tm // 2
    group = max(1, min(n_voc, 192 // rows))
    while n_voc % group:
        group -= 1
    wide = width + LANES
    far_count = max(1, pairs - 1)
    dma = pltpu.SemaphoreType.DMA
    conditioned, logs = pl.pallas_call(
        functools.partial(kernel, n_tm, n_voc, rows, width, hops, group),
        out_shape=(
            jax.ShapeDtypeStruct((rows, width), BF16),
            jax.ShapeDtypeStruct((1, LANES), F32),
        ),
        in_specs=[pl.BlockSpec(memory_space=pl.ANY)] * 5,
        out_specs=(pl.BlockSpec(memory_space=pltpu.VMEM),) * 2,
        scratch_shapes=[
            pltpu.VMEM((hops + 1, rows, width), BF16),
            pltpu.VMEM(qkv_weight.shape, BF16),
            pltpu.VMEM(attn_out_weight.shape, BF16),
            pltpu.VMEM((width, labels), BF16),
            pltpu.VMEM((labels, width), BF16),
            pltpu.VMEM((n_tm, n_voc, rows, width), BF16),
            pltpu.VMEM((n_tm, n_voc, rows, wide), BF16),
            pltpu.VMEM((pairs, n_voc, rows, wide), BF16),
            pltpu.VMEM((far_count, n_voc, rows, wide), BF16),
            pltpu.VMEM((far_count, n_voc, rows, wide), BF16),
            pltpu.VMEM((n_voc - 1, rows, wide), BF16),
            dma((5,)),
            dma((hops,)), dma((hops,)),
            dma((n_tm - 1,)), dma((n_tm - 1,)),
            dma((n_tm - 1,)), dma((n_tm - 1,)),
            dma((n_voc - 1,)), dma((n_voc - 1,)),
            dma((pairs, n_voc)), dma((pairs, n_voc)),
            dma((far_count, n_voc)), dma((far_count, n_voc)),
            dma((pairs,)), dma((pairs,)),
            dma((far_count, n_voc)), dma((far_count, n_voc)),
            dma((n_voc - 1,)), dma((n_voc - 1,)),
        ],
        compiler_params=pltpu.CompilerParams(
            collective_id=0, has_side_effects=True, vmem_limit_bytes=63 * 1024 * 1024
        ),
    )(frames, qkv_weight, attn_out_weight, head_weight, back_weight)
    return conditioned, logs[0, :rows]


def solution(mesh):
    return jax.shard_map(
        functools.partial(body, mesh.shape["tm"], mesh.shape["vocab"]),
        mesh=mesh,
        in_specs=(P(("tm", "vocab"), None), P(), P(), P("tm", "vocab"), P("vocab", "tm")),
        out_specs=(P(("tm", "vocab"), None), P(("tm", "vocab"))),
        check_vma=False,
    )
```

time: 164 us -> 65.2 us (0.40)
  Pallas kernels: 0 us -> 61.9 us
  blocking collectives: 54.2 us -> 0 us
  waiting for transfers between devices: 48.2 us -> 0 us
  starting transfers between devices: 23.3 us -> 0 us
  matrix products: 15.1 us -> 0 us
  between operations: 14.7 us -> 0.64 us
  other arithmetic: 4.91 us -> 0 us
    pallas_call x0 -> x1, Pallas kernels: none -> 61.9 us  [body(): pl.pallas_call(functools.partial(kernel, n_tm, n_voc, rows, width, hops,...]
    reduce_scatter x1 -> x0, waiting for transfers between devices: 39.3 us -> none  [body(): lax.psum_scatter(partial_value, 'vocab', scatter_dimension=0, tiled=True)]
    all_gather x1 -> x0, blocking collectives: 32.7 us -> none  [body(): lax.all_gather(unit, 'vocab', axis=0, tiled=True)]
    ppermute x6 -> x0, starting transfers between devices: 23.2 us -> none  [passed_along(): return lax.ppermute(block, axis, route)]
    unnamed x1 -> x0, blocking collectives: 21.6 us -> none
    dot_general x6 -> x0, matrix products: 15.1 us -> none  [the longest x1 4.05 us: body(): jnp.dot(label_probs, lax.all_gather(back_weight, 'tm', axis=1, tiled=True...]
    all_gather x2 -> x0, waiting for transfers between devices: 5.51 us -> none  [the longest x1 5.51 us: body(): lax.all_gather(back_weight, 'tm', axis=1, tiled=True)]
    reduce_sum x3 -> x0, other arithmetic: 3.09 us -> none  [the longest x1 1.09 us: body(): spread = jnp.mean(center * center, axis=-1, keepdims=True)]
  transfers between devices with their start and end apart: 9 -> 0, of which waited for: 3 -> 0; matrix products, arithmetic and copies ran while one was open for 9% -> 0% of each run, Pallas kernels for 0% -> 0%
where the time goes in v1:
time: 65.2 us; the launch traced here: 65.1 us
  Pallas kernels  61.9 us (95%)
  local copies, waits for them, and re-layouts  2.57 us (4%)
    pallas_call x1, Pallas kernels, body(): pl.pallas_call(functools.partial(kernel, n_tm, n_voc, rows, width, hops,...  61.9 us
    unnamed x1, local copies, waits for them, and re-layouts  1.42 us

profile of v1, /device:TPU:0, one launch (start us, length us, event | category | flops | bytes accessed | tf_op | source)
XLA Modules:
  0.0 65.1 jit_solution(11926086880091399628)
XLA Ops:
  0.6 61.9 %shard_map.68 = (bf16[24,1024]{1,0:T(8,128)(2,1)}, f32[1,128]{1,0:T(1,128)}) custom-call(bf16[24,1024]{1,0:T(8,128)(2,1)} %frames_ref.1, bf16[1024,3072]{1,0:T(8,128)(2,1)} %qkv_ref.1, bf16[1024,1024]{1,0:T(8,128)(2,1)} %out_ref.1, bf16[256,2048]{1,0:T(8,128)(2,1)} %head_ref.1, bf16[2048,256]{1,0:T(8,128)(2,1)} %back_ref.1), custom_call_target="tpu_custom_call" | custom-call | tf_op jit(solution)/shard_map/pallas_call | solution.py:331
  62.5 1.1 %slice_bitcast_fusion = f32[24]{0:T(128)} fusion(f32[1,128]{1,0:T(1,128)} %get-tuple-element.5), kind=kLoop, calls=%fused_computation | loop fusion | bytes 192 | tf_op jit(solution)/shard_map/squeeze | solution.py:366
  63.6 1.4 %copy.8 = bf16[24,1024]{1,0:T(8,128)(2,1)} copy(bf16[24,1024]{1,0:T(8,128)(2,1)} %get-tuple-element.8) | data formatting | bytes 98304

commit v2 on v1

v2 whole, which is shorter than its diff:
```python
import functools
import math

import jax
import jax.numpy as jnp
from jax import lax
from jax.experimental import pallas as pl
from jax.experimental.pallas import tpu as pltpu
from jax.sharding import PartitionSpec as P

HEADS = 16
HEAD_DIM = 64
WIN = 128
LANES = 128
BF16 = jnp.bfloat16
F32 = jnp.float32
MESH = pl.DeviceIdType.MESH


def root_norm(values):
    return values * lax.rsqrt(jnp.mean(values * values, axis=-1, keepdims=True) + 1e-06)


def pack(main, tot):
    lane = lax.broadcasted_iota(jnp.int32, (main.shape[0], LANES), 1)
    high = tot.astype(BF16).astype(F32)
    tail = jnp.where(lane == 0, high, jnp.where(lane == 1, tot - high, 0.0))
    return jnp.concatenate([main, tail], axis=1).astype(BF16)


def unpack(packed, width):
    wide = packed.astype(F32)
    return wide[:, :width], jnp.sum(wide[:, width:], axis=-1, keepdims=True)


def kernel(
    n_tm, n_voc, rows, width, hops, group,
    frames_ref, qkv_ref, out_ref, head_ref, back_ref,
    cond_ref, log_ref,
    fr, wq, wo, head, back, units, parts, near, sums, far, owned, across,
    loc_sem, swap_s, swap_r, halo_s, halo_r, head_s, head_r, back_s, back_r,
    voc_s, voc_r, fwd_s, fwd_r, sib_s, sib_r, near_s, near_r, sum_s, sum_r, acr_s, acr_r, own_s, own_r,
):
    t = lax.axis_index("tm")
    v = lax.axis_index("vocab")
    n_dev = n_tm * n_voc
    pairs = n_tm // 2
    me = t * n_voc + v
    sib = t + 1 - 2 * lax.rem(t, 2)
    depth = head_ref.shape[0]
    labels = head.shape[1]
    chunks = n_voc // group
    half = n_voc // 2
    side = lax.rem(v, 2)
    mate = v + 1 - 2 * side
    lane_pos = v // 2

    def remote(src, dst, ss, rs, dev):
        return pltpu.make_async_remote_copy(
            src_ref=src, dst_ref=dst, send_sem=ss, recv_sem=rs, device_id=dev, device_id_type=MESH
        )

    def other(k):
        return lax.rem(t + k, n_tm)

    def linear(i):
        return (i // n_voc, lax.rem(i, n_voc))

    def head_rows(i):
        return head.at[pl.ds(pl.multiple_of(i * depth, depth), depth)]

    def back_cols(i):
        return back.at[:, pl.ds(pl.multiple_of(i * depth, depth), depth)]

    def head_part(i):
        return head_ref.at[:, pl.ds(pl.multiple_of(i * labels, labels), labels)]

    def back_part(i):
        return back_ref.at[pl.ds(pl.multiple_of(i * labels, labels), labels)]

    local = [
        pltpu.make_async_copy(frames_ref, fr.at[0, hops], loc_sem.at[0]),
        pltpu.make_async_copy(qkv_ref, wq, loc_sem.at[1]),
        pltpu.make_async_copy(out_ref, wo, loc_sem.at[2]),
        pltpu.make_async_copy(head_part(t), head_rows(t), loc_sem.at[3]),
        pltpu.make_async_copy(back_part(t), back_cols(t), loc_sem.at[4]),
    ]
    for copy in local:
        copy.start()

    barrier = pltpu.get_barrier_semaphore()
    greet = lambda dev: pl.semaphore_signal(barrier, inc=1, device_id=dev, device_id_type=MESH)
    for k in range(1, n_tm):
        greet((other(k), v))
    lax.fori_loop(1, n_voc, lambda k, c: (greet((t, lax.rem(v + k, n_voc))), c)[1], 0)
    for s in range(1, hops + 1):
        greet(linear(lax.rem(me + s, n_dev)))
        greet(linear(lax.rem(me + n_dev - s, n_dev)))
    pl.semaphore_wait(barrier, n_tm - 1 + n_voc - 1 + 2 * hops)

    place = [lax.rem(me + 2 * a * n_voc, n_dev) for a in range(pairs)]

    def halo(a, s):
        src = fr.at[a, hops] if a else frames_ref
        return remote(
            src, fr.at[a, hops - s], halo_s.at[a, s - 1], halo_r.at[a, s - 1],
            linear(lax.rem(me + s, n_dev)),
        )

    def start_halo(a):
        for s in range(1, hops + 1):
            @pl.when(place[a] + s < n_dev)
            def _():
                halo(a, s).start()

            @pl.when(place[a] < s)
            def _():
                fr[a, hops - s] = jnp.zeros((rows, width), BF16)

    swaps = [
        remote(frames_ref, fr.at[pairs - a, hops], swap_s.at[pairs - a - 1], swap_r.at[pairs - a - 1], (other(2 * a), v))
        for a in range(1, pairs)
    ]
    for copy in swaps:
        copy.start()
    start_halo(0)

    order = [k for k in range(2, n_tm)] + [1]
    head_copies, back_copies = [], []
    for k in order:
        p = other(k)
        head_copies.append(remote(head_part(p), head_rows(t), head_s.at[k - 1], head_r.at[k - 1], (p, v)))
        back_copies.append(remote(back_part(p), back_cols(t), back_s.at[k - 1], back_r.at[k - 1], (p, v)))
    for copy in head_copies:
        copy.start()
    for copy in swaps:
        copy.wait_recv()
    for a in range(1, pairs):
        start_halo(a)
    for copy in back_copies:
        copy.start()

    local[0].wait()
    used = (hops + 1) * rows
    keys = (used + LANES - 1) // LANES * LANES
    per = LANES // HEAD_DIM
    row = lax.broadcasted_iota(jnp.int32, (rows, keys), 0)
    col = lax.broadcasted_iota(jnp.int32, (rows, keys), 1)
    gap = row + hops * rows - col
    lane = lax.broadcasted_iota(jnp.int32, (rows, LANES), 1)
    local[1].wait()
    local[2].wait()

    def attend(a):
        for s in range(1, hops + 1):
            @pl.when(place[a] >= s)
            def _():
                halo(a, s).wait_recv()

        own = fr[a, hops].astype(F32)
        blocks = [fr[a, i].astype(F32) for i in range(hops)] + [own]
        if keys > used:
            blocks.append(jnp.zeros((keys - used, width), F32))
        normed = root_norm(jnp.concatenate(blocks, axis=0)).astype(BF16)
        query_in = root_norm(own).astype(BF16)
        query = jnp.dot(query_in, wq[:, :width], preferred_element_type=F32)
        key_part = jnp.dot(normed, wq[:, width : 2 * width], preferred_element_type=F32).astype(BF16)
        value_part = jnp.dot(normed, wq[:, 2 * width :], preferred_element_type=F32).astype(BF16)
        allowed = (gap >= 0) & (gap < WIN) & (col + (place[a] - hops) * rows >= 0)
        allowed = jnp.concatenate([allowed.astype(F32)] * per, axis=0) > 0.5
        context = []
        for g in range(width // LANES):
            cols = slice(g * LANES, (g + 1) * LANES)
            q = query[:, cols]
            stacked = jnp.concatenate(
                [jnp.where(lane // HEAD_DIM == h, q, 0.0) for h in range(per)], axis=0
            ).astype(BF16)
            scores = lax.dot_general(
                stacked, key_part[:, cols], (((1,), (1,)), ((), ())), preferred_element_type=F32
            ) / math.sqrt(HEAD_DIM)
            scores = 50.0 * jnp.tanh(scores / 50.0)
            expo = jnp.where(allowed, jnp.exp(scores), 0.0)
            weights = (expo / jnp.sum(expo, axis=-1, keepdims=True)).astype(BF16)
            ctx = jnp.dot(weights, value_part[:, cols], preferred_element_type=F32)
            mixed = ctx[:rows]
            for h in range(1, per):
                mixed = jnp.where(lane // HEAD_DIM == h, ctx[h * rows : (h + 1) * rows], mixed)
            context.append(mixed)
        context = jnp.concatenate(context, axis=1).astype(BF16)
        out = (own + jnp.dot(context, wo[...], preferred_element_type=F32)).astype(BF16).astype(F32)
        units[other(2 * a), v] = root_norm(out).astype(BF16)
        return out

    def spot(k):
        return 2 * lax.rem(lane_pos + k, half) + side

    def voc_copy(a, k):
        o = other(2 * a)
        w = mate if k is None else spot(k)
        i = 0 if k is None else k
        return remote(units.at[o, v], units.at[o, v], voc_s.at[a, i], voc_r.at[a, i], (t, w))

    def fwd_copy(a, k):
        o, w = other(2 * a), spot(half - k)
        return remote(units.at[o, w], units.at[o, w], fwd_s.at[a, k - 1], fwd_r.at[a, k - 1], (t, mate))

    def sib_copy(a, w):
        o = other(2 * a)
        return remote(units.at[o, w], units.at[o, w], sib_s.at[a, w], sib_r.at[a, w], (sib, v))

    def loop(lo, hi, fn):
        def step(i, c):
            fn(i)
            return c

        lax.fori_loop(lo, hi, step, 0)

    def push(a):
        loop(1, half, lambda k: voc_copy(a, k).start())
        voc_copy(a, None).start()
        sib_copy(a, v).start()

    hidden = attend(0)
    push(0)
    for a in range(1, pairs):
        attend(a)
        push(a)
    for a in range(pairs):
        voc_copy(a, None).wait_recv()
        sib_copy(a, mate).start()

        def side_arrived(k):
            voc_copy(a, k).wait_recv()
            fwd_copy(a, k).start()
            sib_copy(a, spot(half - k)).start()

        loop(1, half, side_arrived)

        def mate_arrived(k):
            fwd_copy(a, k).wait_recv()
            sib_copy(a, spot(half - k) + 1 - 2 * side).start()

        loop(1, half, mate_arrived)

    def process(block):
        def chunk(c):
            u = jnp.concatenate(
                [units[block, c * group + j].astype(F32) for j in range(group)], axis=0
            ).astype(BF16)
            logits = jnp.dot(u, head[...], preferred_element_type=F32)
            probs = jnp.exp(30.0 * jnp.tanh(logits / 30.0)).astype(BF16)
            tot = jnp.sum(probs.astype(F32), axis=-1, keepdims=True)
            packed = pack(jnp.dot(probs, back[...], preferred_element_type=F32), tot).astype(F32)
            for j in range(group):
                parts[block, c * group + j] = packed[j * rows : (j + 1) * rows].astype(BF16)

        loop(0, chunks, chunk)

    def near_copy(a):
        return remote(parts.at[lax.rem(sib + 2 * a, n_tm)], near.at[a], near_s.at[a], near_r.at[a], (sib, v))

    local[3].wait()
    for copy in head_copies:
        copy.wait_recv()
    local[4].wait()
    for copy in back_copies:
        copy.wait_recv()
    for a in [*range(1, pairs), 0]:
        process(other(2 * a))
        loop(0, n_voc, lambda w: sib_copy(a, w).wait_recv())
        process(lax.rem(sib + 2 * a, n_tm))
        near_copy(a).start()

    def sum_copy(a, w):
        return remote(
            sums.at[a - 1, w], far.at[a - 1, w], sum_s.at[a - 1, w], sum_r.at[a - 1, w], (other(2 * a), v)
        )

    for a in range(1, pairs):
        near_copy(a).wait_recv()

        def pair_sum(k):
            w = 2 * lax.rem(lane_pos + k // 2, half) + lax.rem(side + 1 + k, 2)
            m0, t0 = unpack(parts[other(2 * a), w], width)
            m1, t1 = unpack(near[a, w], width)
            sums[a - 1, w] = pack(m0 + m1, t0 + t1)
            sum_copy(a, w).start()

        loop(2, n_voc + 2, pair_sum)
    near_copy(0).wait_recv()

    def across_copy(k):
        w = spot(k) + 1 - 2 * side
        return remote(parts.at[t, w], across.at[k - 1], acr_s.at[k - 1], acr_r.at[k - 1], (t, mate))

    def own_copy(k):
        w = spot(k)
        return remote(parts.at[t, w], owned.at[k - 1], own_s.at[k - 1], own_r.at[k - 1], (t, w))

    def tm_sum(w):
        m, s = unpack(parts[t, w], width)
        m1, s1 = unpack(near[0, w], width)
        m, s = m + m1, s + s1
        for a in range(1, pairs):
            sum_copy(a, w).wait_recv()
            m1, s1 = unpack(far[a - 1, w], width)
            m, s = m + m1, s + s1
        return m, s

    def send_across(k):
        w = spot(k) + 1 - 2 * side
        m, s = tm_sum(w)
        parts[t, w] = pack(m, s)
        across_copy(k).start()

    def both_sides(k):
        m, s = tm_sum(spot(k))
        across_copy(k).wait_recv()
        m1, s1 = unpack(across[k - 1], width)
        return m + m1, s + s1

    def send_sum(k):
        send_across(k)
        m, s = both_sides(k)
        parts[t, spot(k)] = pack(m, s)
        own_copy(k).start()

    loop(1, half, send_sum)
    send_across(half)
    total, tot = both_sides(half)
    for k in range(1, half):
        own_copy(k).wait_recv()
        m1, s1 = unpack(owned[k - 1], width)
        total, tot = total + m1, tot + s1
    value = total / tot
    center = value - jnp.mean(value, axis=-1, keepdims=True)
    spread = jnp.mean(center * center, axis=-1, keepdims=True)
    cond_ref[...] = (hidden + center * lax.rsqrt(spread + 1e-05)).astype(BF16)
    r = lax.broadcasted_iota(jnp.int32, (rows, LANES), 0)
    c = lax.broadcasted_iota(jnp.int32, (rows, LANES), 1)
    log_ref[...] = jnp.sum(jnp.where(r == c, jnp.log(tot), 0.0), axis=0, keepdims=True)

    for a in range(pairs):
        for s in range(1, hops + 1):
            @pl.when(place[a] + s < n_dev)
            def _():
                halo(a, s).wait_send()
        voc_copy(a, None).wait_send()

        def sent(k):
            voc_copy(a, k).wait_send()
            fwd_copy(a, k).wait_send()

        loop(1, half, sent)
    for copy in swaps + head_copies + back_copies:
        copy.wait_send()
    loop(1, half, lambda k: own_copy(k).wait_send())
    loop(1, half + 1, lambda k: across_copy(k).wait_send())

    def rest(w):
        for a in range(pairs):
            sib_copy(a, w).wait_send()
            if a:
                sum_copy(a, w).wait_send()

    loop(0, n_voc, rest)
    for a in range(pairs):
        near_copy(a).wait_send()


def body(n_tm, n_voc, frames, qkv_weight, attn_out_weight, head_weight, back_weight):
    rows, width = frames.shape
    hops = (WIN + rows - 1) // rows
    labels = head_weight.shape[1] // n_tm
    pairs = n_tm // 2
    half = n_voc // 2
    group = max(1, min(n_voc, 192 // rows))
    while n_voc % group:
        group -= 1
    wide = width + LANES
    far_count = max(1, pairs - 1)
    dma = pltpu.SemaphoreType.DMA
    conditioned, logs = pl.pallas_call(
        functools.partial(kernel, n_tm, n_voc, rows, width, hops, group),
        out_shape=(
            jax.ShapeDtypeStruct((rows, width), BF16),
            jax.ShapeDtypeStruct((1, LANES), F32),
        ),
        in_specs=[pl.BlockSpec(memory_space=pl.ANY)] * 5,
        out_specs=(pl.BlockSpec(memory_space=pltpu.VMEM),) * 2,
        scratch_shapes=[
            pltpu.VMEM((pairs, hops + 1, rows, width), BF16),
            pltpu.VMEM(qkv_weight.shape, BF16),
            pltpu.VMEM(attn_out_weight.shape, BF16),
            pltpu.VMEM((width, labels), BF16),
            pltpu.VMEM((labels, width), BF16),
            pltpu.VMEM((n_tm, n_voc, rows, width), BF16),
            pltpu.VMEM((n_tm, n_voc, rows, wide), BF16),
            pltpu.VMEM((pairs, n_voc, rows, wide), BF16),
            pltpu.VMEM((far_count, n_voc, rows, wide), BF16),
            pltpu.VMEM((far_count, n_voc, rows, wide), BF16),
            pltpu.VMEM((half, rows, wide), BF16),
            pltpu.VMEM((half, rows, wide), BF16),
            dma((5,)),
            dma((far_count,)), dma((far_count,)),
            dma((pairs, hops)), dma((pairs, hops)),
            dma((n_tm - 1,)), dma((n_tm - 1,)),
            dma((n_tm - 1,)), dma((n_tm - 1,)),
            dma((pairs, half)), dma((pairs, half)),
            dma((pairs, half)), dma((pairs, half)),
            dma((pairs, n_voc)), dma((pairs, n_voc)),
            dma((pairs,)), dma((pairs,)),
            dma((far_count, n_voc)), dma((far_count, n_voc)),
            dma((half,)), dma((half,)),
            dma((half,)), dma((half,)),
        ],
        compiler_params=pltpu.CompilerParams(
            collective_id=0, has_side_effects=True, vmem_limit_bytes=63 * 1024 * 1024
        ),
    )(frames, qkv_weight, attn_out_weight, head_weight, back_weight)
    return conditioned, logs[0, :rows]


def solution(mesh):
    return jax.shard_map(
        functools.partial(body, mesh.shape["tm"], mesh.shape["vocab"]),
        mesh=mesh,
        in_specs=(P(("tm", "vocab"), None), P(), P(), P("tm", "vocab"), P("vocab", "tm")),
        out_specs=(P(("tm", "vocab"), None), P(("tm", "vocab"))),
        check_vma=False,
    )
```

time: 65.2 us -> 68.1 us (1.044)
  Pallas kernels: 61.9 us -> 64.7 us
    pallas_call x1, Pallas kernels: 61.9 us -> 64.7 us  [body(): pl.pallas_call(functools.partial(kernel, n_tm, n_voc, rows, width, hops,...]
where the time goes in v2:
time: 68.1 us; the launch traced here: 67.9 us
  Pallas kernels  64.7 us (95%)
  local copies, waits for them, and re-layouts  2.57 us (4%)
    pallas_call x1, Pallas kernels, body(): pl.pallas_call(functools.partial(kernel, n_tm, n_voc, rows, width, hops,...  64.7 us
    unnamed x1, local copies, waits for them, and re-layouts  1.42 us

profile of v2, /device:TPU:0, one launch (start us, length us, event | category | flops | bytes accessed | tf_op | source)
XLA Modules:
  0.0 67.9 jit_solution(11668453694475007975)
XLA Ops:
  0.6 64.7 %shard_map.68 = (bf16[24,1024]{1,0:T(8,128)(2,1)}, f32[1,128]{1,0:T(1,128)}) custom-call(bf16[24,1024]{1,0:T(8,128)(2,1)} %frames_ref.1, bf16[1024,3072]{1,0:T(8,128)(2,1)} %qkv_ref.1, bf16[1024,1024]{1,0:T(8,128)(2,1)} %out_ref.1, bf16[256,2048]{1,0:T(8,128)(2,1)} %head_ref.1, bf16[2048,256]{1,0:T(8,128)(2,1)} %back_ref.1), custom_call_target="tpu_custom_call" | custom-call | tf_op jit(solution)/shard_map/pallas_call | solution.py:383
  65.4 1.1 %slice_bitcast_fusion = f32[24]{0:T(128)} fusion(f32[1,128]{1,0:T(1,128)} %get-tuple-element.5), kind=kLoop, calls=%fused_computation | loop fusion | bytes 192 | tf_op jit(solution)/shard_map/squeeze | solution.py:421
  66.5 1.4 %copy.8 = bf16[24,1024]{1,0:T(8,128)(2,1)} copy(bf16[24,1024]{1,0:T(8,128)(2,1)} %get-tuple-element.8) | data formatting | bytes 98304
